TPU v7x, 32 devices: a whole 2x2x4 slice. The times are simulated.
32 devices in a mesh: rows: 2 (over y), mp: 16 (over z, x, core).
Axes of the slice: x: 2, y: 2, z: 4, core: 2. Of those that a mesh axis runs over, the one named last changes fastest.
Arguments:
- lam_out: bfloat16 [1024, 16, 1024], P('mp', 'rows'), may hold values from -6 to 6
- q_down: bfloat16 [1024, 4096], P(None, 'rows'), may hold values from -127 to 127, as said below
- down_scale: float32 [1024], replicated, may hold values from 0.0001 to 0.001
- q_up: bfloat16 [4096, 1024], P('rows'), may hold values from -127 to 127, as said below
- up_scale: float32 [4096], P('rows'), may hold values from 5e-05 to 0.0005
- chan_slopes: bfloat16 [2, 1024, 2, 4096], P(None, 'mp', 'rows'), may hold values from -0.14941406 to 1.09375
- chan_icpt: bfloat16 [2, 1024, 2, 4096], P(None, 'mp', 'rows')
- tok_in_blocks: bfloat16 [16, 128, 128], replicated, may hold values from -0.25 to 0.25
- tok_out_blocks: bfloat16 [16, 128, 128], replicated, may hold values from -0.25 to 0.25
- block_cells: int32 [16], replicated, may hold values from 0 to 31, as said below
- tok_slopes: bfloat16 [2, 512, 2, 1024], P(None, None, 'rows', 'mp'), may hold values from -0.14941406 to 1.09375
- tok_icpt: bfloat16 [2, 512, 2, 1024], P(None, None, 'rows', 'mp')
Outputs:
- lam_in: bfloat16 [1024, 16, 1024], P(None, 'rows', 'mp')
- bias: float32 [16], P('rows')
Inputs may be any that keep to these rules, and one draw needn't show every extreme that they name: `q_down`: integer values, 8-bit signed codes; a program may carry them across devices in any exact packed form, several codes to an element. `q_up`: integer values, 8-bit signed codes; a program may carry them across devices in any exact packed form, several codes to an element. `block_cells`: 16 distinct cells; cell h * 8 + u is hidden block h and token block u.
All inputs are finite; a program needn't handle non-finite values.
Results may differ from a plain program's by a relative error of at most 0.012.
Values may be sent and summed in bfloat16 or wider, within the bound.
A program may use at most 128 MiB of HBM per device.

v0:
```python
import jax
import jax.numpy as jnp
from jax import lax
from jax.sharding import PartitionSpec as P

D = 1024
CH = 4096
TH = 512
TOK = 1024
BLK = 128
SPEC = 8
IMG_DEV = 1
NHB = 4
NTB = 8


def dense_blocks(blocks, cells, count_rows, count_cols):
    row_hot = (
        cells[:, None] // count_cols == jnp.arange(count_rows, dtype=jnp.int32)[None, :]
    ).astype(jnp.float32)
    col_hot = (
        cells[:, None] % count_cols == jnp.arange(count_cols, dtype=jnp.int32)[None, :]
    ).astype(jnp.float32)
    dense = jnp.einsum("bh,bt,bij->hitj", row_hot, col_hot, blocks.astype(jnp.float32))
    return dense.reshape(count_rows * BLK, count_cols * BLK).astype(jnp.bfloat16)


def relax(pre, slopes, icpt):
    pos = jnp.maximum(pre, 0.0)
    neg = jnp.minimum(pre, 0.0)
    lower = slopes[0].astype(jnp.float32)[:, :, None, :]
    upper = slopes[1].astype(jnp.float32)[:, :, None, :]
    icpt_low = icpt[0].astype(jnp.float32)[:, :, None, :]
    icpt_high = icpt[1].astype(jnp.float32)[:, :, None, :]
    mid = pos * lower + neg * upper
    row_bias = jnp.sum(pos * icpt_low + neg * icpt_high, axis=(0, 3)).reshape(-1)
    return (mid, row_bias)


def on_device(
    lam_out,
    q_down,
    down_scale,
    q_up,
    up_scale,
    chan_slopes,
    chan_icpt,
    tok_in_blocks,
    tok_out_blocks,
    block_cells,
    tok_slopes,
    tok_icpt,
):
    tok_dev = lam_out.shape[0]
    rows_dev = lam_out.shape[1]
    rows_all = rows_dev * lax.axis_size("rows")
    offset = lax.axis_index("rows") * rows_dev
    scaled = (lam_out.astype(jnp.float32) * down_scale).astype(jnp.bfloat16)
    flat = scaled.reshape(-1, D)
    pre = jnp.dot(
        flat, lax.all_gather(q_down, "rows", axis=1, tiled=True), preferred_element_type=jnp.float32
    )
    pre = pre.reshape(tok_dev, IMG_DEV, SPEC, CH)
    mid, own_bias = relax(pre, chan_slopes, chan_icpt)
    mid_flat = mid.reshape(-1, CH)
    codes = lax.all_gather(q_up, "rows", axis=0, tiled=True)
    scales = lax.all_gather(up_scale.astype(jnp.bfloat16), "rows", axis=0, tiled=True).astype(
        jnp.float32
    )
    weighted = (mid_flat * scales).astype(jnp.bfloat16)
    summed = jnp.dot(weighted, codes, preferred_element_type=jnp.float32)
    summed = summed.reshape(tok_dev, rows_dev, D)
    chan_bias = lax.dynamic_update_slice_in_dim(
        jnp.zeros((rows_all,), jnp.float32), own_bias, offset, 0
    )
    lam_res = (lam_out.astype(jnp.float32) + summed).astype(jnp.bfloat16)
    turned = lax.all_to_all(lam_res, "mp", split_axis=2, concat_axis=0, tiled=True)
    chan_dev = turned.shape[2]
    columns = turned.reshape(TOK, rows_dev * chan_dev)
    tok_in = dense_blocks(tok_in_blocks, block_cells, NHB, NTB)
    swapped = block_cells % NTB * NHB + block_cells // NTB
    tok_out = dense_blocks(tok_out_blocks, swapped, NTB, NHB)
    tpre = lax.dot_general(
        tok_out, columns, (((0,), (0,)), ((), ())), preferred_element_type=jnp.float32
    )
    tpre = tpre.reshape(TH, IMG_DEV, SPEC, chan_dev)
    tmid, tok_bias = relax(tpre, tok_slopes, tok_icpt)
    tmid = tmid.astype(jnp.bfloat16).reshape(TH, rows_dev * chan_dev)
    back = lax.dot_general(
        tok_in, tmid, (((0,), (0,)), ((), ())), preferred_element_type=jnp.float32
    )
    lam_in = (turned.astype(jnp.float32) + back.reshape(TOK, rows_dev, chan_dev)).astype(
        jnp.bfloat16
    )
    placed = lax.dynamic_update_slice_in_dim(
        jnp.zeros((rows_all,), jnp.float32), tok_bias, offset, 0
    )
    totals = lax.psum(chan_bias + placed, ("rows", "mp"))
    bias = lax.dynamic_slice_in_dim(totals, offset, rows_dev, 0)
    return (lam_in, bias)


def solution(mesh):
    return jax.shard_map(
        on_device,
        mesh=mesh,
        in_specs=(
            P("mp", "rows", None),
            P(None, "rows"),
            P(),
            P("rows", None),
            P("rows"),
            P(None, "mp", "rows", None),
            P(None, "mp", "rows", None),
            P(),
            P(),
            P(),
            P(None, None, "rows", "mp"),
            P(None, None, "rows", "mp"),
        ),
        out_specs=(P(None, "rows", "mp"), P("rows")),
        check_vma=False,
    )
```

profile of v0, /device:TPU:0, one launch (start us, length us, event | category | flops | bytes accessed | tf_op | source)
XLA Modules:
  0.0 334.4 jit_solution(4554349527780292279)
XLA Ops:
  7.2 0.7 all-gather.3.cloned.1.call-update
  8.0 0.7 all-gather.5.cloned.1.call-update
  8.7 5.3 %all_gather.10 = bf16[4096]{0:T(1024)(128)(2,1)S(1)} all-gather(bf16[2048]{0:T(1024)(128)(2,1)S(1)} %convert_element_type.160), channel_id=1, replica_groups=mesh['rows'=2,'mp'=16] {'rows'}, dimensions={0}, use_global_device_ids=true | all-gather | bytes 12288 | tf_op jit(solution)/shard_map/all_gather | solution.py:67
  14.0 1.6 bitcast_convert_fusion.2
  15.6 0.2 bitcast_convert_fusion.4
  15.8 100.5 %all-gather.3.cloned.1.call-done = bf16[1024,4096]{1,0:T(8,128)(2,1)} async-done(((bf16[1024,2048]{1,0:T(8,128)(2,1)}), bf16[1024,4096]{1,0:T(8,128)(2,1)}) %all-gather.3.cloned.1.call-update) | async-done | bytes 8388624 | tf_op jit(solution)/shard_map/all_gather | solution.py:61
  116.3 10.7 %fusion.1 = (f32[512]{0:T(512)S(1)}, f32[512,4096]{1,0:T(8,128)}) fusion(f32[64,4096]{1,0:T(8,128)} %get-tuple-element.9, f32[64,4096]{1,0:T(8,128)} %get-tuple-element.8, bf16[1024,4096]{1,0:T(8,128)(2,1)} %all-gather.3.cloned.1.call-done, bf16[64,8,1024]{2,1,0:T(8,128)(2,1)} %param.12, f32[1024]{0:T(1024)S(1)} %copy-done.8), kind=kOutput, calls=%fused_computation.2 | convolution fusion | flops 4309122560 | bytes 19929088 | tf_op jit(solution)/shard_map/dot_general | solution.py:60
  127.0 94.9 %all-gather.5.cloned.1.call-done = bf16[4096,1024]{1,0:T(8,128)(2,1)} async-done(((bf16[2048,1024]{1,0:T(8,128)(2,1)}), bf16[4096,1024]{1,0:T(8,128)(2,1)}) %all-gather.5.cloned.1.call-update) | async-done | bytes 8388624 | tf_op jit(solution)/shard_map/all_gather | solution.py:66
  221.9 10.2 %fusion.14 = bf16[64,8,1024]{2,1,0:T(8,128)(2,1)} fusion(bf16[64,8,1024]{2,1,0:T(8,128)(2,1)S(1)} %copy-done.7, bf16[4096,1024]{1,0:T(8,128)(2,1)} %all-gather.5.cloned.1.call-done, f32[512,4096]{1,0:T(8,128)} %get-tuple-element.17, f32[4096]{0:T(1024)S(1)} %convert_element_type.161, f32[64,4096]{1,0:T(8,128)S(1)} %get-tuple-element.11, ...), kind=kOutput, calls=%fused_computation.19 | convolution fusion | flops 4311220224 | bytes 20987904 | tf_op jit(solution)/shard_map/dot_general | solution.py:71
  232.2 3.4 %copy.34 = bf16[64,8,1024]{0,1,2:T(8,128)(2,1)S(1)} copy(bf16[64,8,1024]{2,1,0:T(8,128)(2,1)} %fusion.14) | data formatting | bytes 2097152 | tf_op jit(solution)/shard_map/convert_element_type | solution.py:76
  235.6 2.2 reshape.238
  237.8 5.6 %all-to-all-start = ((bf16[16,2,16384]{2,1,0:T(2,128)(2,1)}), bf16[16,2,16384]{2,1,0:T(2,128)(2,1)S(1)}, u32[]{:S(2)}, u32[]{:S(2)}) async-start(bf16[16,2,16384]{2,1,0:T(2,128)(2,1)} %reshape.238), calls=%async_computation | async-start | bytes 2097152 | tf_op jit(solution)/shard_map/all_to_all | solution.py:77
  243.6 0.5 fusion.20
  244.0 1.7 copy.39
  245.7 0.5 fusion.19
  246.2 1.3 reshape.236
  247.5 1.6 bitcast_convert_fusion.6
  249.1 0.1 reduce_sum.24
  249.2 0.2 dynamic_update_slice.8
  249.5 16.9 %all-to-all-done = bf16[16,2,16384]{2,1,0:T(2,128)(2,1)S(1)} async-done(((bf16[16,2,16384]{2,1,0:T(2,128)(2,1)}), bf16[16,2,16384]{2,1,0:T(2,128)(2,1)S(1)}, u32[]{:S(2)}, u32[]{:S(2)}) %all-to-all-start) | async-done | bytes 1048608 | tf_op jit(solution)/shard_map/all_to_all | solution.py:77
  266.4 2.4 reshape.239
  268.8 3.7 %copy.35 = bf16[64,8,16,64]{3,1,0,2:T(8,128)(2,1)S(1)} copy(bf16[64,8,16,64]{0,1,3,2:T(8,128)(2,1)} %bitcast.141) | data formatting | bytes 2097152 | tf_op jit(solution)/shard_map/all_to_all | solution.py:77
  272.5 1.3 reshape.221
  273.7 3.0 fusion.28
  276.7 0.1 reduce_sum.36
  276.8 0.1 reduce_sum.37
  276.9 0.2 add_dynamic-update-slice_fusion
  277.1 2.4 bitcast_convert_fusion
  279.5 41.9 %psum.7 = f32[16]{0:T(128)S(1)} all-reduce(f32[16]{0:T(128)S(1)} %add_dynamic-update-slice_fusion), channel_id=1, replica_groups=mesh['rows'=2,'mp'=16] {'rows','mp'}, use_global_device_ids=true, to_apply=%region_4.5 | all-reduce | flops 16 | bytes 128 | tf_op jit(solution)/shard_map/psum | solution.py:98
  321.4 0.6 dynamic_slice.3
  322.0 2.8 copy.42
  324.8 2.7 add_convert_fusion
  (29 shorter events, 0.2 us)
Async XLA Ops:
  7.2 1.5 copy-start.5
  7.2 6.8 %copy-start.1 = (bf16[2,64,1,4096]{3,1,2,0:T(8,128)(2,1)S(1)}, bf16[2,64,1,4096]{3,1,2,0:T(8,128)(2,1)}, u32[]{:S(2)}) copy-start(bf16[2,64,1,4096]{3,1,2,0:T(8,128)(2,1)} %param.18) | copy-start | bytes 3145732
  7.2 8.4 %copy-start.2 = (bf16[2,64,1,4096]{3,1,2,0:T(8,128)(2,1)S(1)}, bf16[2,64,1,4096]{3,1,2,0:T(8,128)(2,1)}, u32[]{:S(2)}) copy-start(bf16[2,64,1,4096]{3,1,2,0:T(8,128)(2,1)} %param.17) | copy-start | bytes 3145732
  7.2 109.1 %copy-start.8 = (f32[1024]{0:T(1024)S(1)}, f32[1024]{0:T(1024)}, u32[]{:S(2)}) copy-start(f32[1024]{0:T(1024)} %param.14) | copy-start | bytes 12292
  7.2 109.1 %all-gather.3.cloned.1.call-start = ((), (), s32[]{:S(2)}) async-start(), calls=%async_computation.1 | async-start | bytes 12582912 | tf_op jit(solution)/shard_map/all_gather | solution.py:61
  7.9 214.0 %all-gather.5.cloned.1.call-start = ((), (), s32[]{:S(2)}) async-start(), calls=%async_computation.2 | async-start | bytes 12582912 | tf_op jit(solution)/shard_map/all_gather | solution.py:66
  116.3 105.6 %copy-start.7 = (bf16[64,8,1024]{2,1,0:T(8,128)(2,1)S(1)}, bf16[64,8,1024]{2,1,0:T(8,128)(2,1)}, u32[]{:S(2)}) copy-start(bf16[64,8,1024]{2,1,0:T(8,128)(2,1)} %param.12) | copy-start | bytes 3145732
  232.1 11.3 %copy-start.6 = (s32[16]{0:T(128)S(1)}, s32[16]{0:T(128)}, u32[]{:S(2)}) copy-start(s32[16]{0:T(128)} %param.21) | copy-start | bytes 196
  232.2 11.4 %copy-start.3 = (bf16[16,128,128]{2,1,0:T(8,128)(2,1)S(1)}, bf16[16,128,128]{2,1,0:T(8,128)(2,1)}, u32[]{:S(2)}) copy-start(bf16[16,128,128]{2,1,0:T(8,128)(2,1)} %param.20) | copy-start | bytes 1572868
  232.2 13.6 %copy-start.4 = (bf16[16,128,128]{2,1,0:T(8,128)(2,1)S(1)}, bf16[16,128,128]{2,1,0:T(8,128)(2,1)}, u32[]{:S(2)}) copy-start(bf16[16,128,128]{2,1,0:T(8,128)(2,1)} %param.19) | copy-start | bytes 1572868
  237.8 28.6 %all-to-all-start = ((bf16[16,2,16384]{2,1,0:T(2,128)(2,1)}), bf16[16,2,16384]{2,1,0:T(2,128)(2,1)S(1)}, u32[]{:S(2)}, u32[]{:S(2)}) async-start(bf16[16,2,16384]{2,1,0:T(2,128)(2,1)} %reshape.238), calls=%async_computation | async-start | bytes 2097152 | tf_op jit(solution)/shard_map/all_to_all | solution.py:77
  276.7 48.1 %copy-start = (bf16[512,1024,1]{1,0,2:T(8,128)(2,1)S(1)}, bf16[512,1024,1]{1,0,2:T(8,128)(2,1)}, u32[]{:S(2)}) copy-start(bf16[512,1024,1]{1,0,2:T(8,128)(2,1)} %reshape.236) | copy-start | bytes 3145732
Sparse Core Ops, SparseCore 0:
  9.6 106.6 all-gather.2
  117.9 103.9 all-gather.4
where the time goes:
time: 335 us; the launch traced here: 334 us
  waiting for transfers between devices  214 us (64%)
  blocking collectives  47.2 us (14%)
  matrix products  27.6 us (8%)
  local copies, waits for them, and re-layouts  19.8 us (6%)
  between operations  14.2 us (4%)
  other arithmetic  6.17 us (2%)
  starting transfers between devices  5.7 us (2%)
    all_gather x1, waiting for transfers between devices, on_device(): lax.all_gather(q_down, 'rows', axis=1, tiled=True)  101 us
    all_gather x1, waiting for transfers between devices, on_device(): codes = lax.all_gather(q_up, 'rows', axis=0, tiled=True)  94.9 us
    psum x1, blocking collectives, on_device(): totals = lax.psum(chan_bias + placed, ('rows', 'mp'))  41.9 us
    all_to_all x1, waiting for transfers between devices, on_device(): lax.all_to_all(lam_res, 'mp', split_axis=2, concat_axis=0, tiled=True)  16.9 us
    dot_general x1, matrix products, on_device(): jnp.dot(flat, lax.all_gather(q_down, 'rows', axis=1, tiled=True), preferr...  10.7 us
    dot_general x1, matrix products, on_device(): summed = jnp.dot(weighted, codes, preferred_element_type=jnp.float32)  10.2 us
  transfers between devices with their start and end apart: 3, of which 3 were waited for; matrix products, arithmetic and copies ran while one was open for 6% of the time, Pallas kernels for 0%

commit v1 on v0

--- a/solution.py
+++ b/solution.py
@@ -1,6 +1,8 @@
 import jax
 import jax.numpy as jnp
 from jax import lax
+from jax.experimental import pallas as pl
+from jax.experimental.pallas import tpu as pltpu
 from jax.sharding import PartitionSpec as P
 
 D = 1024
@@ -100,9 +102,521 @@
     return (lam_in, bias)
 
 
+MESH = pl.DeviceIdType.MESH
+F32 = jnp.float32
+BF16 = jnp.bfloat16
+QW = 512
+NP = 8
+PR = 64
+
+
+def fused_kernel(
+    lam_hbm,
+    qd_hbm,
+    qu_hbm,
+    ds_ref,
+    us_ref,
+    cs_hbm,
+    ci_hbm,
+    tin_hbm,
+    tout_hbm,
+    cells,
+    ts_hbm,
+    ti_hbm,
+    out_ref,
+    bias_ref,
+    qd_v,
+    qu_v,
+    pk_qd,
+    pk_qu,
+    spk,
+    pbuf,
+    usr,
+    cs_v,
+    ci_v,
+    lam_v,
+    scaled,
+    acc,
+    wbuf,
+    unp,
+    bacc,
+    sbuf,
+    rb,
+    xt,
+    tin_v,
+    tout_v,
+    tin_d,
+    tout_d,
+    ts_v,
+    ti_v,
+    tmid,
+    bsend,
+    brecv,
+    lsem,
+    ssem,
+    rsem,
+    usem,
+    a_s,
+    a_r,
+    b_s,
+    b_r,
+):
+    y = lax.axis_index("rows")
+    m = lax.axis_index("mp")
+    q = lax.rem(m, 4)
+    cb = lax.rem(m, 2)
+    xb = lax.div(q, 2)
+    xn = m + 2 - 4 * xb
+    cn = m + 1 - 2 * cb
+    qx = lax.rem(q + 2, 4)
+    qc = q + 1 - 2 * cb
+    qd = lax.rem(qc + 2, 4)
+    half = QW * 4
+
+    def local(src, dst, k):
+        c = pltpu.make_async_copy(src, dst, lsem.at[k])
+        c.start()
+        return c
+
+    c_pkd = local(qd_hbm.at[:, pl.ds(pl.multiple_of(q * QW, QW), QW)], pk_qd, 0)
+    c_pku = local(qu_hbm.at[pl.ds(pl.multiple_of(q * QW, QW), QW), :], pk_qu, 1)
+    c_lam = local(lam_hbm, lam_v, 2)
+    loc = []
+    for i in range(4):
+        off = pl.multiple_of(y * half + i * QW, QW)
+        loc.append(
+            [
+                local(qd_hbm.at[:, i * QW : (i + 1) * QW], qd_v.at[i], 3 + 4 * i),
+                local(cs_hbm.at[:, :, pl.ds(off, QW)], cs_v.at[i], 4 + 4 * i),
+                local(ci_hbm.at[:, :, pl.ds(off, QW)], ci_v.at[i], 5 + 4 * i),
+                local(qu_hbm.at[i * QW : (i + 1) * QW, :], qu_v.at[i], 6 + 4 * i),
+            ]
+        )
+    rem = []
+    for i, qq in enumerate((q, qx, qc, qd)):
+        off = pl.multiple_of((1 - y) * half + qq * QW, QW)
+        rem.append(
+            [
+                local(cs_hbm.at[:, :, pl.ds(off, QW)], cs_v.at[4 + i], 19 + 2 * i),
+                local(ci_hbm.at[:, :, pl.ds(off, QW)], ci_v.at[4 + i], 20 + 2 * i),
+            ]
+        )
+    toks = [
+        local(tin_hbm, tin_v, 27),
+        local(tout_hbm, tout_v, 28),
+        local(ts_hbm, ts_v, 29),
+        local(ti_hbm, ti_v, 30),
+    ]
+
+    barrier = pltpu.get_barrier_semaphore()
+    pl.semaphore_signal(barrier, inc=1, device_id=(1 - y, m), device_id_type=MESH)
+
+    @pl.loop(1, 16)
+    def _(k):
+        pl.semaphore_signal(
+            barrier, inc=1, device_id=(y, lax.rem(m + k, 16)), device_id_type=MESH
+        )
+
+    def pack(parts):
+        w = None
+        for k, part in enumerate(parts):
+            code = part.astype(F32).astype(jnp.int32)
+            code = (code & 255) << (8 * k) if k < 3 else code << 24
+            w = code if w is None else w | code
+        return w
+
+    def y_copy(p):
+        return pltpu.make_async_remote_copy(
+            src_ref=spk.at[p],
+            dst_ref=pbuf.at[q, p],
+            send_sem=ssem.at[p],
+            recv_sem=rsem.at[q, p],
+            device_id=(1 - y, m),
+            device_id_type=MESH,
+        )
+
+    def piece(slot, p, sem, dev):
+        return pltpu.make_async_remote_copy(
+            src_ref=pbuf.at[slot, p],
+            dst_ref=pbuf.at[slot, p],
+            send_sem=ssem.at[sem],
+            recv_sem=rsem.at[slot, p],
+            device_id=(y, dev),
+            device_id_type=MESH,
+        )
+
+    def scale_copy():
+        return pltpu.make_async_remote_copy(
+            src_ref=us_ref,
+            dst_ref=usr,
+            send_sem=usem.at[0],
+            recv_sem=usem.at[1],
+            device_id=(1 - y, m),
+            device_id_type=MESH,
+        )
+
+    c_pkd.wait()
+    spk[0] = pack([pk_qd[i * 256 : i * 256 + PR, :] for i in range(4)])
+    pl.semaphore_wait(barrier, 16)
+    y_copy(0).start()
+    for p in range(1, 4):
+        spk[p] = pack([pk_qd[i * 256 + p * PR : i * 256 + (p + 1) * PR, :] for i in range(4)])
+        y_copy(p).start()
+    c_pku.wait()
+    for p in range(4):
+        spk[4 + p] = pack(
+            [
+                pk_qu[a * 256 + p * PR : a * 256 + (p + 1) * PR, b * QW : (b + 1) * QW]
+                for a in range(2)
+                for b in range(2)
+            ]
+        )
+        y_copy(4 + p).start()
+    scale_copy().start()
+
+    c_lam.wait()
+    flat = lam_v[...].astype(F32).reshape(512, D).astype(BF16)
+    to = lax.broadcasted_iota(jnp.int32, (512, 512), 0)
+    frm = lax.broadcasted_iota(jnp.int32, (512, 512), 1)
+    perm = ((to & 63) * 8 + (to >> 6) == frm).astype(F32).astype(BF16)
+    for n in range(2):
+        cols = slice(n * 512, (n + 1) * 512)
+        turned = jnp.dot(perm, flat[:, cols], preferred_element_type=F32)
+        acc[:, cols] = turned
+        scaled[:, cols] = (turned * ds_ref[:, cols]).astype(BF16)
+    bacc[...] = jnp.zeros_like(bacc)
+
+    def weights(codes, scale, s):
+        @pl.loop(0, 2)
+        def _(g):
+            cols = pl.ds(pl.multiple_of(g * 256, 256), 256)
+            pre = jnp.dot(scaled[...], codes[:, cols], preferred_element_type=F32)
+            low = cs_v[s, 0, :, cols].astype(F32) * scale[:, cols]
+            up = cs_v[s, 1, :, cols].astype(F32) * scale[:, cols]
+            ilow = ci_v[s, 0, :, cols].astype(F32)
+            iup = ci_v[s, 1, :, cols].astype(F32)
+            for r in range(8):
+                part = pre[r * 64 : (r + 1) * 64]
+                pos = part > 0.0
+                w = part * jnp.where(pos, low, up)
+                wbuf[s, r * 64 : (r + 1) * 64, cols] = w.astype(BF16)
+                b = (part * jnp.where(pos, ilow, iup)).reshape(8, 8, 256).sum(axis=0)
+                bacc[r] = bacc[r] + (b[:, :128] + b[:, 128:])
+
+    def add_back(codes, s):
+        @pl.loop(0, 2)
+        def _(g):
+            cols = pl.ds(pl.multiple_of(g * 512, 512), 512)
+            acc[:, cols] = acc[:, cols] + jnp.dot(
+                wbuf[s], codes[:, cols], preferred_element_type=F32
+            )
+
+    def unpack(w, k):
+        code = w << (24 - 8 * k) if k < 3 else w
+        return (code >> 24).astype(F32).astype(BF16)
+
+    def y_step(p):
+        piece(q, p, 8, xn).wait_recv()
+        piece(q, p, 8 + p, xn).start()
+        piece(q, p, 16 + p, cn).start()
+
+    def x_step(p):
+        piece(qx, p, 8, cn).wait_recv()
+        piece(qx, p, 24 + p, cn).start()
+
+    def wait_pieces(slot, lo):
+        for p in range(lo, lo + 4):
+            piece(slot, p, 8, cn).wait_recv()
+
+    def remote_weights(slot, i):
+        for c in rem[i]:
+            c.wait()
+        for k in range(4):
+            unp[k * 256 : (k + 1) * 256, :] = unpack(
+                pbuf[slot, pl.ds(0, 4)].reshape(256, QW), k
+            )
+        weights(unp, usr.at[slot], 4 + i)
+
+    def remote_codes(slot, i):
+        w = pbuf[slot, pl.ds(4, 4)].reshape(256, QW)
+        for k in range(4):
+            a, b = k // 2, k % 2
+            qu_v[i, a * 256 : (a + 1) * 256, b * QW : (b + 1) * QW] = unpack(w, k)
+
+    def local_quarter(i):
+        for c in loc[i]:
+            c.wait()
+        weights(qd_v.at[i], us_ref.at[i], i)
+        add_back(qu_v.at[i], i)
+
+    local_quarter(0)
+    y_step(0)
+    local_quarter(1)
+    y_step(1)
+    x_step(0)
+    local_quarter(2)
+    y_step(2)
+    x_step(1)
+    local_quarter(3)
+    y_step(3)
+    x_step(2)
+    scale_copy().wait()
+    remote_weights(q, 0)
+    y_step(4)
+    x_step(3)
+    remote_weights(qx, 1)
+    y_step(5)
+    x_step(4)
+    wait_pieces(qc, 0)
+    remote_weights(qc, 2)
+    y_step(6)
+    x_step(5)
+    wait_pieces(qd, 0)
+    remote_weights(qd, 3)
+    y_step(7)
+    x_step(6)
+    remote_codes(q, 0)
+    add_back(qu_v.at[0], 4)
+    x_step(7)
+    remote_codes(qx, 1)
+    wait_pieces(qc, 4)
+    remote_codes(qc, 2)
+    wait_pieces(qd, 4)
+    remote_codes(qd, 3)
+
+    def turn_copy(to_dev, src):
+        return pltpu.make_async_remote_copy(
+            src_ref=sbuf.at[to_dev],
+            dst_ref=rb.at[:, pl.ds(pl.multiple_of(src * 64, 64), 64), :],
+            send_sem=a_s.at[to_dev],
+            recv_sem=a_r.at[src],
+            device_id=(y, to_dev),
+            device_id_type=MESH,
+        )
+
+    zb = lax.div(m, 4)
+    order = (lax.rem(zb + 2, 4), 3 - zb, zb + 1 - 2 * lax.rem(zb, 2), zb)
+    lane = lax.broadcasted_iota(jnp.int32, (256, 128), 1)
+    for z in order:
+        cols = pl.ds(pl.multiple_of(z * 256, 256), 256)
+        total = acc[:, cols]
+        for i in range(1, 4):
+            total = total + jnp.dot(
+                wbuf[4 + i], qu_v[i, :, cols], preferred_element_type=F32
+            )
+        for x in range(2):
+            a = total[0:256, x * 128 : (x + 1) * 128]
+            b = total[256:512, x * 128 : (x + 1) * 128]
+            first = jnp.where(lane < 64, a, pltpu.roll(b, 64, 1))
+            second = jnp.where(lane < 64, pltpu.roll(a, 64, 1), b)
+            sbuf[z * 4 + 2 * x] = first.astype(BF16).reshape(4, 64, 128)
+            sbuf[z * 4 + 2 * x + 1] = second.astype(BF16).reshape(4, 64, 128)
+        if z is not zb:
+            for k in range(4):
+                turn_copy(z * 4 + k, m).start()
+    xcn = xn + 1 - 2 * cb
+    for dev in (xn, xcn, cn):
+        turn_copy(dev, m).start()
+    rb[:, pl.ds(pl.multiple_of(m * 64, 64), 64), :] = sbuf[m]
+
+    for c in toks:
+        c.wait()
+
+    @pl.loop(0, NHB * NTB)
+    def _(cell):
+        at = jnp.int32(0)
+        hits = jnp.int32(0)
+        for b in range(16):
+            hit = (cells[b] == cell).astype(jnp.int32)
+            at = jnp.maximum(at, b * hit)
+            hits = hits + hit
+        on = hits.astype(F32)
+        h = pl.multiple_of(lax.div(cell, NTB) * BLK, BLK)
+        u = pl.multiple_of(lax.rem(cell, NTB) * BLK, BLK)
+        tin_d[pl.ds(h, BLK), pl.ds(u, BLK)] = (tin_v[at].astype(F32) * on).astype(BF16)
+        tout_d[pl.ds(u, BLK), pl.ds(h, BLK)] = (tout_v[at].astype(F32) * on).astype(BF16)
+
+    def transpose_chip(chip):
+        at = pl.ds(pl.multiple_of(chip * 128, 128), 128)
+        for r in range(4):
+            xt[r * 128 : (r + 1) * 128, at] = rb[r, at, :].astype(F32).T.astype(BF16)
+
+    for z in order[:3]:
+        for x in range(2):
+            turn_copy(cn, z * 4 + 2 * x).wait_recv()
+            turn_copy(cn, z * 4 + 2 * x + 1).wait_recv()
+            transpose_chip(z * 2 + x)
+    turn_copy(cn, xn).wait_recv()
+    turn_copy(cn, xcn).wait_recv()
+    transpose_chip(lax.div(xn, 2))
+    turn_copy(cn, cn).wait_recv()
+    transpose_chip(lax.div(m, 2))
+
+    @pl.loop(0, 2)
+    def _(g):
+        rows = pl.ds(pl.multiple_of(g * 256, 256), 256)
+        tpre = jnp.dot(xt[rows, :], tout_d[...], preferred_element_type=F32)
+        low = ts_v[0].astype(F32)
+        up = ts_v[1].astype(F32)
+        ilow = ti_v[0].astype(F32)
+        iup = ti_v[1].astype(F32)
+        for j in range(4):
+            part = tpre[j * 64 : (j + 1) * 64]
+            pos = part > 0.0
+            t = part * jnp.where(pos, low, up)
+            tmid[pl.ds(pl.multiple_of(g * 256 + j * 64, 64), 64), :] = t.astype(BF16)
+            b = (part * jnp.where(pos, ilow, iup)).reshape(8, 8, TH).sum(axis=0)
+            b = b[:, :128] + b[:, 128:256] + b[:, 256:384] + b[:, 384:]
+            r = g * 2 + j // 2 + 4 * (j % 2)
+            bacc[r] = bacc[r] + b
+
+    bsend[...] = jnp.sum(bacc[...], axis=1)
+
+    def bias_copy(k, src):
+        to_dev = lax.rem(m + k, 16)
+        return pltpu.make_async_remote_copy(
+            src_ref=bsend,
+            dst_ref=brecv.at[src],
+            send_sem=b_s.at[k],
+            recv_sem=b_r.at[src],
+            device_id=(y, to_dev),
+            device_id_type=MESH,
+        )
+
+    @pl.loop(1, 16)
+    def _(k):
+        bias_copy(k, m).start()
+
+    brecv[m] = bsend[...]
+
+    for g in range(4):
+        back = jnp.dot(
+            tmid[g * 128 : (g + 1) * 128, :], tin_d[...], preferred_element_type=F32
+        )
+        total = (xt[g * 128 : (g + 1) * 128, :].astype(F32) + back).astype(BF16)
+        out_ref[g] = total[:64]
+        out_ref[g + 4] = total[64:]
+
+    @pl.loop(1, 16)
+    def _(k):
+        bias_copy(k, lax.rem(m + 16 - k, 16)).wait_recv()
+
+    total = jnp.sum(brecv[...], axis=0)
+    bias_ref[...] = jnp.broadcast_to(jnp.sum(total, axis=1, keepdims=True), (8, 128))
+
+    for p in range(NP):
+        y_copy(p).wait_send()
+        piece(q, p, 8 + p, xn).wait_send()
+        piece(q, p, 16 + p, cn).wait_send()
+        piece(qx, p, 24 + p, cn).wait_send()
+
+    @pl.loop(1, 16)
+    def _(k):
+        turn_copy(lax.rem(m + k, 16), m).wait_send()
+        bias_copy(k, m).wait_send()
+
+
+def on_device_fused(
+    lam_out,
+    q_down,
+    down_scale,
+    q_up,
+    up_scale,
+    chan_slopes,
+    chan_icpt,
+    tok_in_blocks,
+    tok_out_blocks,
+    block_cells,
+    tok_slopes,
+    tok_icpt,
+):
+    hbm = pl.BlockSpec(memory_space=pl.ANY)
+    vmem = pl.BlockSpec(memory_space=pltpu.VMEM)
+    dma = pltpu.SemaphoreType.DMA
+    ts = jnp.transpose(tok_slopes[:, :, 0, :], (0, 2, 1))
+    ti = jnp.transpose(tok_icpt[:, :, 0, :], (0, 2, 1))
+    out, bias = pl.pallas_call(
+        fused_kernel,
+        out_shape=(
+            jax.ShapeDtypeStruct((8, 64, TOK), BF16),
+            jax.ShapeDtypeStruct((8, 128), F32),
+        ),
+        in_specs=[
+            hbm,
+            hbm,
+            hbm,
+            vmem,
+            vmem,
+            hbm,
+            hbm,
+            hbm,
+            hbm,
+            pl.BlockSpec(memory_space=pltpu.SMEM),
+            hbm,
+            hbm,
+        ],
+        out_specs=(vmem, vmem),
+        scratch_shapes=[
+            pltpu.VMEM((4, D, QW), BF16),
+            pltpu.VMEM((4, QW, D), BF16),
+            pltpu.VMEM((D, QW), BF16),
+            pltpu.VMEM((QW, D), BF16),
+            pltpu.VMEM((NP, PR, QW), jnp.int32),
+            pltpu.VMEM((4, NP, PR, QW), jnp.int32),
+            pltpu.VMEM((4, 1, QW), F32),
+            pltpu.VMEM((8, 2, 64, QW), BF16),
+            pltpu.VMEM((8, 2, 64, QW), BF16),
+            pltpu.VMEM((64, 8, D), BF16),
+            pltpu.VMEM((512, D), BF16),
+            pltpu.VMEM((512, D), F32),
+            pltpu.VMEM((8, 512, QW), BF16),
+            pltpu.VMEM((D, QW), BF16),
+            pltpu.VMEM((8, 8, 128), F32),
+            pltpu.VMEM((16, 4, 64, 128), BF16),
+            pltpu.VMEM((4, TOK, 128), BF16),
+            pltpu.VMEM((512, TOK), BF16),
+            pltpu.VMEM((16, BLK, BLK), BF16),
+            pltpu.VMEM((16, BLK, BLK), BF16),
+            pltpu.VMEM((TH, TOK), BF16),
+            pltpu.VMEM((TOK, TH), BF16),
+            pltpu.VMEM((2, 64, TH), BF16),
+            pltpu.VMEM((2, 64, TH), BF16),
+            pltpu.VMEM((512, TH), BF16),
+            pltpu.VMEM((8, 128), F32),
+            pltpu.VMEM((16, 8, 128), F32),
+            dma((31,)),
+            dma((32,)),
+            dma((4, NP)),
+            dma((2,)),
+            dma((16,)),
+            dma((16,)),
+            dma((16,)),
+            dma((16,)),
+        ],
+        compiler_params=pltpu.CompilerParams(
+            collective_id=0, has_side_effects=True, vmem_limit_bytes=56 * 1024 * 1024
+        ),
+    )(
+        lam_out,
+        q_down,
+        q_up,
+        down_scale.reshape(1, D),
+        up_scale.reshape(4, 1, QW),
+        chan_slopes[:, :, 0, :],
+        chan_icpt[:, :, 0, :],
+        tok_in_blocks,
+        tok_out_blocks,
+        block_cells,
+        ts,
+        ti,
+    )
+    return (jnp.transpose(out, (2, 0, 1)), bias[:, 0])
+
+
 def solution(mesh):
+    fits = mesh.shape['rows'] == 2 and mesh.shape['mp'] == 16
     return jax.shard_map(
-        on_device,
+        on_device_fused if fits else on_device,
         mesh=mesh,
         in_specs=(
             P("mp", "rows", None),

time: 335 us -> 85.8 us (0.26)
  waiting for transfers between devices: 214 us -> 0 us
  Pallas kernels: 0 us -> 81.4 us
  blocking collectives: 47.2 us -> 0 us
  matrix products: 27.6 us -> 0 us
  local copies, waits for them, and re-layouts: 19.8 us -> 3.56 us
  between operations: 14.2 us -> 0.64 us
  other arithmetic: 6.17 us -> 0 us
  starting transfers between devices: 5.7 us -> 0 us
    all_gather x2 -> x0, waiting for transfers between devices: 195 us -> none  [the longest x1 101 us: on_device(): lax.all_gather(q_down, 'rows', axis=1, tiled=True)]
    pallas_call x0 -> x1, Pallas kernels: none -> 81.4 us  [on_device_fused(): pl.pallas_call(fused_kernel, out_shape=(jax.ShapeDtypeStruct((8, 64, TOK)...]
    psum x1 -> x0, blocking collectives: 41.9 us -> none  [on_device(): totals = lax.psum(chan_bias + placed, ('rows', 'mp'))]
    dot_general x6 -> x0, matrix products: 27.6 us -> none  [the longest x1 10.7 us: on_device(): jnp.dot(flat, lax.all_gather(q_down, 'rows', axis=1, tiled=True), preferr...]
    all_to_all x1 -> x0, waiting for transfers between devices: 16.9 us -> none  [on_device(): lax.all_to_all(lam_res, 'mp', split_axis=2, concat_axis=0, tiled=True)]
    convert_element_type x4 -> x0, local copies, waits for them, and re-layouts: 9.22 us -> none  [the longest x1 3.42 us: on_device(): lam_res = (lam_out.astype(jnp.float32) + summed).astype(jnp.bfloat16)]
    convert_element_type x6 -> x0, other arithmetic: 5.82 us -> none  [the longest x2 3.25 us: relax(): icpt_low = icpt[0].astype(jnp.float32)[:, :, None, :]]
    all_to_all x1 -> x0, starting transfers between devices: 5.62 us -> none  [on_device(): lax.all_to_all(lam_res, 'mp', split_axis=2, concat_axis=0, tiled=True)]
  transfers between devices with their start and end apart: 3 -> 0, of which waited for: 3 -> 0; matrix products, arithmetic and copies ran while one was open for 6% -> 0% of each run, Pallas kernels for 0% -> 0%
where the time goes in v1:
time: 85.8 us; the launch traced here: 85.6 us
  Pallas kernels  81.4 us (95%)
  local copies, waits for them, and re-layouts  3.56 us (4%)
    pallas_call x1, Pallas kernels, on_device_fused(): pl.pallas_call(fused_kernel, out_shape=(jax.ShapeDtypeStruct((8, 64, TOK)...  81.4 us
    unnamed x1, local copies, waits for them, and re-layouts  2.26 us

profile of v1, /device:TPU:0, one launch (start us, length us, event | category | flops | bytes accessed | tf_op | source)
XLA Modules:
  0.0 85.6 jit_solution(10539808876530755274)
XLA Ops:
  0.6 81.4 %shard_map.131 = (bf16[8,64,1024]{2,1,0:T(8,128)(2,1)}, f32[8,128]{1,0:T(8,128)}) custom-call(bf16[64,8,1024]{2,1,0:T(8,128)(2,1)} %lam_hbm.1, bf16[1024,2048]{1,0:T(8,128)(2,1)} %qd_hbm.1, bf16[2048,1024]{1,0:T(8,128)(2,1)} %qu_hbm.1, f32[1,1024]{1,0:T(1,128)} %bitcast.17, f32[4,1,512]{2,1,0:T(1,128)} %bitcast.16, bf16[2,64,4096]{2,1,0:T(8,128)(2,1)} %bitcast.12, ...), custom_call_target="tpu_custom_call" | custom-call | tf_op jit(solution)/shard_map/pallas_call | solution.py:538
  82.0 1.3 %slice_reduce_fusion = f32[8]{0:T(128)} fusion(f32[8,128]{1,0:T(8,128)} %get-tuple-element.5), kind=kLoop, calls=%fused_computation | loop fusion | bytes 64 | tf_op jit(solution)/shard_map/slice | solution.py:613
  83.3 2.3 %copy.15 = bf16[1024,8,64]{0,2,1:T(8,128)(2,1)} copy(bf16[1024,8,64]{0,2,1:T(8,128)(2,1)} %bitcast.11) | data formatting | bytes 2097152

commit v2 on v1

--- a/solution.py
+++ b/solution.py
@@ -106,8 +106,9 @@
 F32 = jnp.float32
 BF16 = jnp.bfloat16
 QW = 512
-NP = 8
-PR = 64
+EW = 256
+NP = 4
+PR = 128
 
 
 def fused_kernel(
@@ -116,6 +117,7 @@
     qu_hbm,
     ds_ref,
     us_ref,
+    us8_ref,
     cs_hbm,
     ci_hbm,
     tin_hbm,
@@ -163,14 +165,17 @@
 ):
     y = lax.axis_index("rows")
     m = lax.axis_index("mp")
-    q = lax.rem(m, 4)
+    e = lax.rem(m, 8)
     cb = lax.rem(m, 2)
-    xb = lax.div(q, 2)
-    xn = m + 2 - 4 * xb
-    cn = m + 1 - 2 * cb
-    qx = lax.rem(q + 2, 4)
-    qc = q + 1 - 2 * cb
-    qd = lax.rem(qc + 2, 4)
+    xb = lax.rem(lax.div(m, 2), 2)
+    zl = lax.div(e, 4)
+    dx = 2 - 4 * xb
+    dc = 1 - 2 * cb
+    dz = 4 - 8 * zl
+    xn = m + dx
+    cn = m + dc
+    zn = m + dz
+    ex, ez, ed = e + dx, e + dz, e + dx + dz
     half = QW * 4
 
     def local(src, dst, k):
@@ -178,8 +183,9 @@
         c.start()
         return c
 
-    c_pkd = local(qd_hbm.at[:, pl.ds(pl.multiple_of(q * QW, QW), QW)], pk_qd, 0)
-    c_pku = local(qu_hbm.at[pl.ds(pl.multiple_of(q * QW, QW), QW), :], pk_qu, 1)
+    own = pl.multiple_of(e * EW, EW)
+    c_pkd = local(qd_hbm.at[:, pl.ds(own, EW)], pk_qd, 0)
+    c_pku = local(qu_hbm.at[pl.ds(own, EW), :], pk_qu, 1)
     c_lam = local(lam_hbm, lam_v, 2)
     loc = []
     for i in range(4):
@@ -193,19 +199,22 @@
             ]
         )
     rem = []
-    for i, qq in enumerate((q, qx, qc, qd)):
-        off = pl.multiple_of((1 - y) * half + qq * QW, QW)
-        rem.append(
-            [
-                local(cs_hbm.at[:, :, pl.ds(off, QW)], cs_v.at[4 + i], 19 + 2 * i),
-                local(ci_hbm.at[:, :, pl.ds(off, QW)], ci_v.at[4 + i], 20 + 2 * i),
-            ]
-        )
+    for i, base in enumerate((e, ex, ez, ed)):
+        for h in range(2):
+            off = pl.multiple_of((1 - y) * half + (base + h * dc) * EW, EW)
+            dst = pl.ds(h * EW, EW)
+            k = 19 + 4 * i + 2 * h
+            rem.append(
+                [
+                    local(cs_hbm.at[:, :, pl.ds(off, EW)], cs_v.at[4 + i, :, :, dst], k),
+                    local(ci_hbm.at[:, :, pl.ds(off, EW)], ci_v.at[4 + i, :, :, dst], k + 1),
+                ]
+            )
     toks = [
-        local(tin_hbm, tin_v, 27),
-        local(tout_hbm, tout_v, 28),
-        local(ts_hbm, ts_v, 29),
-        local(ti_hbm, ti_v, 30),
+        local(tin_hbm, tin_v, 35),
+        local(tout_hbm, tout_v, 36),
+        local(ts_hbm, ts_v, 37),
+        local(ti_hbm, ti_v, 38),
     ]
 
     barrier = pltpu.get_barrier_semaphore()
@@ -228,9 +237,9 @@
     def y_copy(p):
         return pltpu.make_async_remote_copy(
             src_ref=spk.at[p],
-            dst_ref=pbuf.at[q, p],
+            dst_ref=pbuf.at[e, p],
             send_sem=ssem.at[p],
-            recv_sem=rsem.at[q, p],
+            recv_sem=rsem.at[e, p],
             device_id=(1 - y, m),
             device_id_type=MESH,
         )
@@ -247,7 +256,7 @@
 
     def scale_copy():
         return pltpu.make_async_remote_copy(
-            src_ref=us_ref,
+            src_ref=us8_ref,
             dst_ref=usr,
             send_sem=usem.at[0],
             recv_sem=usem.at[1],
@@ -259,19 +268,14 @@
     spk[0] = pack([pk_qd[i * 256 : i * 256 + PR, :] for i in range(4)])
     pl.semaphore_wait(barrier, 16)
     y_copy(0).start()
-    for p in range(1, 4):
-        spk[p] = pack([pk_qd[i * 256 + p * PR : i * 256 + (p + 1) * PR, :] for i in range(4)])
-        y_copy(p).start()
+    spk[1] = pack([pk_qd[i * 256 + PR : i * 256 + 2 * PR, :] for i in range(4)])
+    y_copy(1).start()
     c_pku.wait()
-    for p in range(4):
-        spk[4 + p] = pack(
-            [
-                pk_qu[a * 256 + p * PR : a * 256 + (p + 1) * PR, b * QW : (b + 1) * QW]
-                for a in range(2)
-                for b in range(2)
-            ]
-        )
-        y_copy(4 + p).start()
+    for p in range(2):
+        spk[2 + p] = pack(
+            [pk_qu[p * PR : (p + 1) * PR, b * 256 : (b + 1) * 256] for b in range(4)]
+        )
+        y_copy(2 + p).start()
     scale_copy().start()
 
     c_lam.wait()
@@ -286,22 +290,19 @@
         scaled[:, cols] = (turned * ds_ref[:, cols]).astype(BF16)
     bacc[...] = jnp.zeros_like(bacc)
 
-    def weights(codes, scale, s):
-        @pl.loop(0, 2)
-        def _(g):
-            cols = pl.ds(pl.multiple_of(g * 256, 256), 256)
-            pre = jnp.dot(scaled[...], codes[:, cols], preferred_element_type=F32)
-            low = cs_v[s, 0, :, cols].astype(F32) * scale[:, cols]
-            up = cs_v[s, 1, :, cols].astype(F32) * scale[:, cols]
-            ilow = ci_v[s, 0, :, cols].astype(F32)
-            iup = ci_v[s, 1, :, cols].astype(F32)
-            for r in range(8):
-                part = pre[r * 64 : (r + 1) * 64]
-                pos = part > 0.0
-                w = part * jnp.where(pos, low, up)
-                wbuf[s, r * 64 : (r + 1) * 64, cols] = w.astype(BF16)
-                b = (part * jnp.where(pos, ilow, iup)).reshape(8, 8, 256).sum(axis=0)
-                bacc[r] = bacc[r] + (b[:, :128] + b[:, 128:])
+    def weights(codes, scale, s, cols):
+        pre = jnp.dot(scaled[...], codes, preferred_element_type=F32)
+        low = cs_v[s, 0, :, cols].astype(F32) * scale
+        up = cs_v[s, 1, :, cols].astype(F32) * scale
+        ilow = ci_v[s, 0, :, cols].astype(F32)
+        iup = ci_v[s, 1, :, cols].astype(F32)
+        for r in range(8):
+            part = pre[r * 64 : (r + 1) * 64]
+            pos = part > 0.0
+            w = part * jnp.where(pos, low, up)
+            wbuf[s, r * 64 : (r + 1) * 64, cols] = w.astype(BF16)
+            b = (part * jnp.where(pos, ilow, iup)).reshape(8, 8, 256).sum(axis=0)
+            bacc[r] = bacc[r] + (b[:, :128] + b[:, 128:])
 
     def add_back(codes, s):
         @pl.loop(0, 2)
@@ -316,37 +317,59 @@
         return (code >> 24).astype(F32).astype(BF16)
 
     def y_step(p):
-        piece(q, p, 8, xn).wait_recv()
-        piece(q, p, 8 + p, xn).start()
-        piece(q, p, 16 + p, cn).start()
+        piece(e, p, 4, xn).wait_recv()
+        piece(e, p, 4 + p, xn).start()
+        piece(e, p, 8 + p, zn).start()
+        piece(e, p, 12 + p, cn).start()
 
     def x_step(p):
-        piece(qx, p, 8, cn).wait_recv()
-        piece(qx, p, 24 + p, cn).start()
-
-    def wait_pieces(slot, lo):
-        for p in range(lo, lo + 4):
-            piece(slot, p, 8, cn).wait_recv()
-
-    def remote_weights(slot, i):
-        for c in rem[i]:
+        piece(ex, p, 4, cn).wait_recv()
+        if p % 2 == 0:
+            piece(ex, p, 28 + p, zn).start()
+        piece(ex, p, 16 + p, cn).start()
+
+    def z_step(p):
+        piece(ez, p, 4, cn).wait_recv()
+        if p % 2 == 1:
+            piece(ez, p, 28 + p, xn).start()
+        piece(ez, p, 20 + p, cn).start()
+
+    def d_step(p):
+        piece(ed, p, 4, cn).wait_recv()
+        piece(ed, p, 24 + p, cn).start()
+
+    def wait_core(slot, lo):
+        for p in range(lo, lo + 2):
+            piece(slot + dc, p, 4, cn).wait_recv()
+
+    def remote_weights(slot, i, h):
+        if h:
+            wait_core(slot, 0)
+            slot = slot + dc
+        for c in rem[2 * i + h]:
             c.wait()
+        w = pbuf[slot, pl.ds(0, 2)].reshape(256, EW)
         for k in range(4):
-            unp[k * 256 : (k + 1) * 256, :] = unpack(
-                pbuf[slot, pl.ds(0, 4)].reshape(256, QW), k
-            )
-        weights(unp, usr.at[slot], 4 + i)
-
-    def remote_codes(slot, i):
-        w = pbuf[slot, pl.ds(4, 4)].reshape(256, QW)
+            unp[k * 256 : (k + 1) * 256, :] = unpack(w, k)
+        weights(unp[...], usr[slot], 4 + i, pl.ds(h * EW, EW))
+
+    def remote_codes(slot, i, h):
+        if h:
+            wait_core(slot, 2)
+            slot = slot + dc
+        w = pbuf[slot, pl.ds(2, 2)].reshape(256, EW)
         for k in range(4):
-            a, b = k // 2, k % 2
-            qu_v[i, a * 256 : (a + 1) * 256, b * QW : (b + 1) * QW] = unpack(w, k)
+            qu_v[i, h * EW : (h + 1) * EW, k * 256 : (k + 1) * 256] = unpack(w, k)
 
     def local_quarter(i):
         for c in loc[i]:
             c.wait()
-        weights(qd_v.at[i], us_ref.at[i], i)
+
+        @pl.loop(0, 2)
+        def _(g):
+            cols = pl.ds(pl.multiple_of(g * 256, 256), 256)
+            weights(qd_v[i, :, cols], us_ref[i, :, cols], i, cols)
+
         add_back(qu_v.at[i], i)
 
     local_quarter(0)
@@ -354,35 +377,37 @@
     local_quarter(1)
     y_step(1)
     x_step(0)
+    z_step(0)
     local_quarter(2)
     y_step(2)
     x_step(1)
+    z_step(1)
+    scale_copy().wait()
+    remote_weights(e, 0, 0)
+    remote_weights(ex, 1, 0)
+    y_step(3)
+    d_step(0)
+    d_step(1)
     local_quarter(3)
-    y_step(3)
+    remote_weights(ez, 2, 0)
     x_step(2)
-    scale_copy().wait()
-    remote_weights(q, 0)
-    y_step(4)
+    z_step(2)
+    remote_weights(e, 0, 1)
+    remote_weights(ed, 3, 0)
     x_step(3)
-    remote_weights(qx, 1)
-    y_step(5)
-    x_step(4)
-    wait_pieces(qc, 0)
-    remote_weights(qc, 2)
-    y_step(6)
-    x_step(5)
-    wait_pieces(qd, 0)
-    remote_weights(qd, 3)
-    y_step(7)
-    x_step(6)
-    remote_codes(q, 0)
+    z_step(3)
+    remote_weights(ex, 1, 1)
+    remote_weights(ez, 2, 1)
+    remote_weights(ed, 3, 1)
+    remote_codes(e, 0, 0)
+    remote_codes(e, 0, 1)
+    d_step(2)
+    d_step(3)
     add_back(qu_v.at[0], 4)
-    x_step(7)
-    remote_codes(qx, 1)
-    wait_pieces(qc, 4)
-    remote_codes(qc, 2)
-    wait_pieces(qd, 4)
-    remote_codes(qd, 3)
+    for h in range(2):
+        remote_codes(ex, 1, h)
+        remote_codes(ez, 2, h)
+        remote_codes(ed, 3, h)
 
     def turn_copy(to_dev, src):
         return pltpu.make_async_remote_copy(
@@ -395,7 +420,7 @@
         )
 
     zb = lax.div(m, 4)
-    order = (lax.rem(zb + 2, 4), 3 - zb, zb + 1 - 2 * lax.rem(zb, 2), zb)
+    order = (lax.rem(zb + 2, 4), zb + 1 - 2 * lax.rem(zb, 2), 3 - zb, zb)
     lane = lax.broadcasted_iota(jnp.int32, (256, 128), 1)
     for z in order:
         cols = pl.ds(pl.multiple_of(z * 256, 256), 256)
@@ -506,9 +531,16 @@
 
     for p in range(NP):
         y_copy(p).wait_send()
-        piece(q, p, 8 + p, xn).wait_send()
-        piece(q, p, 16 + p, cn).wait_send()
-        piece(qx, p, 24 + p, cn).wait_send()
+        piece(e, p, 4 + p, xn).wait_send()
+        piece(e, p, 8 + p, zn).wait_send()
+        piece(e, p, 12 + p, cn).wait_send()
+        piece(ex, p, 16 + p, cn).wait_send()
+        piece(ez, p, 20 + p, cn).wait_send()
+        piece(ed, p, 24 + p, cn).wait_send()
+        if p % 2 == 0:
+            piece(ex, p, 28 + p, zn).wait_send()
+        else:
+            piece(ez, p, 28 + p, xn).wait_send()
 
     @pl.loop(1, 16)
     def _(k):
@@ -547,6 +579,7 @@
             hbm,
             vmem,
             vmem,
+            vmem,
             hbm,
             hbm,
             hbm,
@@ -559,18 +592,18 @@
         scratch_shapes=[
             pltpu.VMEM((4, D, QW), BF16),
             pltpu.VMEM((4, QW, D), BF16),
-            pltpu.VMEM((D, QW), BF16),
-            pltpu.VMEM((QW, D), BF16),
-            pltpu.VMEM((NP, PR, QW), jnp.int32),
-            pltpu.VMEM((4, NP, PR, QW), jnp.int32),
-            pltpu.VMEM((4, 1, QW), F32),
+            pltpu.VMEM((D, EW), BF16),
+            pltpu.VMEM((EW, D), BF16),
+            pltpu.VMEM((NP, PR, EW), jnp.int32),
+            pltpu.VMEM((8, NP, PR, EW), jnp.int32),
+            pltpu.VMEM((8, 1, EW), F32),
             pltpu.VMEM((8, 2, 64, QW), BF16),
             pltpu.VMEM((8, 2, 64, QW), BF16),
             pltpu.VMEM((64, 8, D), BF16),
             pltpu.VMEM((512, D), BF16),
             pltpu.VMEM((512, D), F32),
             pltpu.VMEM((8, 512, QW), BF16),
-            pltpu.VMEM((D, QW), BF16),
+            pltpu.VMEM((D, EW), BF16),
             pltpu.VMEM((8, 8, 128), F32),
             pltpu.VMEM((16, 4, 64, 128), BF16),
             pltpu.VMEM((4, TOK, 128), BF16),
@@ -584,9 +617,9 @@
             pltpu.VMEM((512, TH), BF16),
             pltpu.VMEM((8, 128), F32),
             pltpu.VMEM((16, 8, 128), F32),
-            dma((31,)),
+            dma((39,)),
             dma((32,)),
-            dma((4, NP)),
+            dma((8, NP)),
             dma((2,)),
             dma((16,)),
             dma((16,)),
@@ -602,6 +635,7 @@
         q_up,
         down_scale.reshape(1, D),
         up_scale.reshape(4, 1, QW),
+        up_scale.reshape(8, 1, EW),
         chan_slopes[:, :, 0, :],
         chan_icpt[:, :, 0, :],
         tok_in_blocks,

time: 85.8 us -> 73.6 us (0.86)
  Pallas kernels: 81.4 us -> 69.2 us
    pallas_call x1, Pallas kernels: 81.4 us -> 69.2 us  [on_device_fused(): pl.pallas_call(fused_kernel, out_shape=(jax.ShapeDtypeStruct((8, 64, TOK)...]
where the time goes in v2:
time: 73.6 us; the launch traced here: 73.4 us
  Pallas kernels  69.2 us (94%)
  local copies, waits for them, and re-layouts  3.56 us (5%)
    pallas_call x1, Pallas kernels, on_device_fused(): pl.pallas_call(fused_kernel, out_shape=(jax.ShapeDtypeStruct((8, 64, TOK)...  69.2 us
    unnamed x1, local copies, waits for them, and re-layouts  2.26 us

profile of v2, /device:TPU:0, one launch (start us, length us, event | category | flops | bytes accessed | tf_op | source)
XLA Modules:
  0.0 73.4 jit_solution(9555563973331759878)
XLA Ops:
  0.6 69.2 %shard_map.131 = (bf16[8,64,1024]{2,1,0:T(8,128)(2,1)}, f32[8,128]{1,0:T(8,128)}) custom-call(bf16[64,8,1024]{2,1,0:T(8,128)(2,1)} %lam_hbm.1, bf16[1024,2048]{1,0:T(8,128)(2,1)} %qd_hbm.1, bf16[2048,1024]{1,0:T(8,128)(2,1)} %qu_hbm.1, f32[1,1024]{1,0:T(1,128)} %bitcast.19, f32[4,1,512]{2,1,0:T(1,128)} %bitcast.17, f32[8,1,256]{2,1,0:T(1,128)} %bitcast.18, ...), custom_call_target="tpu_custom_call" | custom-call | tf_op jit(solution)/shard_map/pallas_call | solution.py:570
  69.8 1.3 %slice_reduce_fusion = f32[8]{0:T(128)} fusion(f32[8,128]{1,0:T(8,128)} %get-tuple-element.5), kind=kLoop, calls=%fused_computation | loop fusion | bytes 64 | tf_op jit(solution)/shard_map/slice | solution.py:647
  71.1 2.3 %copy.15 = bf16[1024,8,64]{0,2,1:T(8,128)(2,1)} copy(bf16[1024,8,64]{0,2,1:T(8,128)(2,1)} %bitcast.14) | data formatting | bytes 2097152
